TPU v7x, 256 devices: a whole 4x4x8 slice. The times are simulated.
256 devices in a mesh: batch: 32 (over z, x), head: 8 (over y, core).
Axes of the slice: x: 4, y: 4, z: 8, core: 2. Of those that a mesh axis runs over, the one named last changes fastest.
Arguments:
- queries: bfloat16 [4096, 2, 8192], P(('batch', 'head')), may hold values from -48 to 48
- new_kv: bfloat16 [4096, 2, 2, 1024], P('batch', None, None, 'head'), may hold values from -22 to 22
- suffix_cache: bfloat16 [4096, 2, 128, 1024], P('batch', None, None, 'head'), may hold values from -9 to 9
- prefix_cache: bfloat16 [32, 2, 1536, 1024], P('batch', None, None, 'head'), may hold values from -6 to 6
- sample_prompt: int32 [4096, 1], P('batch'), may hold values from 0 to 31; in each aligned block of 128 rows (0 to 127, 128 to 255, ...) at most 8 rows name the same one
- prefix_slot: int32 [32], replicated, may hold values from 0 to 31, each once
- suffix_len: int32 [4096], P('batch'), may hold values from 32 to 128, as said below
Outputs:
- attended: bfloat16 [4096, 2, 8192], P(('batch', 'head'))
Inputs may be any that keep to these rules, and one draw needn't show every extreme that they name: `sample_prompt`: in the rows of one device (aligned blocks of 128 samples) no prompt is named by more than 8 samples; in some block one prompt is named by exactly 8. `prefix_slot`: each prompt has its own storage row. `suffix_len`: in each aligned block of 128 samples the first has 128.
All inputs are finite; a program needn't handle non-finite values.
Results may differ from a plain program's by a relative error of at most 0.0035.
Values may be sent and summed in bfloat16 or wider, within the bound.
No kernel may reach another device: no remote copies, remote signals or barrier semaphores. Data moves between devices by JAX's collectives and lax.ppermute only.
A program may use at most 128 MiB of HBM per device.

v0:
```python
import functools

import jax
import jax.numpy as jnp
from jax import lax
from jax.experimental import pallas as pl
from jax.experimental.pallas import tpu as pltpu
from jax.sharding import PartitionSpec as P

QH = 64
KVH = 8
HD = 128
GQ = QH // KVH
ROWS = 2 * GQ
STAT = 16
SCALE = HD ** (-0.5)
LOG2E = 1.4426950408889634
XS = 4
VMEM = 48 * 1024 * 1024


def nt(a, b):
    return lax.dot_general(a, b, (((1,), (1,)), ((), ())), preferred_element_type=jnp.float32)


def slots_kernel(cap, home_ref, prompt_ref, place_ref, slot_ref, count_ref):
    def clear(j, _):
        count_ref[j] = 0
        return 0

    lax.fori_loop(0, place_ref.shape[0], clear, 0)
    home_x = home_ref[0] % XS

    def assign(s, _):
        storage = place_ref[prompt_ref[s]]
        rank = count_ref[storage]
        count_ref[storage] = rank + 1
        near_by = (storage + (XS - home_x)) % XS
        slot_ref[s] = (storage // XS * XS + near_by) * cap + rank
        return 0

    lax.fori_loop(0, prompt_ref.shape[0], assign, 0)


def pack_kernel(slot_ref, query_ref, left_ref, right_ref, packed_ref):
    del left_ref, right_ref
    packed_ref[...] = jnp.zeros_like(packed_ref)

    def put(s, _):
        source = pl.multiple_of(s * ROWS, ROWS)
        target = pl.multiple_of(slot_ref[s] * ROWS, ROWS)
        packed_ref[pl.ds(target, ROWS), :] = query_ref[pl.ds(source, ROWS), :]
        return 0

    lax.fori_loop(0, slot_ref.shape[0], put, 0, unroll=8)


def near_kernel(per, len_ref, query_ref, cache_ref, key_ref, value_ref, out_ref, lse_ref):
    step = pl.program_id(0)
    rows = per * ROWS
    query = query_ref[...]
    lane = lax.broadcasted_iota(jnp.int32, (ROWS, HD), 1)
    scores = []
    for j in range(per):
        part = nt(query[j * ROWS : (j + 1) * ROWS], cache_ref[j, 0])
        scores.append(jnp.where(lane < len_ref[step * per + j], part, -1e30))
    old = jnp.concatenate(scores, axis=0)
    group = HD // 2
    row = lax.broadcasted_iota(jnp.int32, (rows, HD), 0)
    col = lax.broadcasted_iota(jnp.int32, (rows, HD), 1)
    owner = lax.rem(step, group // per) * per + lax.shift_right_logical(row, 4)
    seen = jnp.logical_and(
        lax.shift_right_logical(col, 1) == owner, (col & 1) <= (row & 1)
    )
    fresh = jnp.where(seen, nt(query, key_ref[...]), -1e30)
    peak = jnp.max(jnp.maximum(old, fresh), axis=1, keepdims=True)
    old_weights = jnp.exp((old - peak) * SCALE).astype(jnp.bfloat16)
    fresh_weights = jnp.exp((fresh - peak) * SCALE).astype(jnp.bfloat16)
    total = jnp.sum(
        old_weights.astype(jnp.float32) + fresh_weights.astype(jnp.float32), axis=1, keepdims=True
    )
    sums = [
        jnp.dot(
            old_weights[j * ROWS : (j + 1) * ROWS],
            cache_ref[j, 1],
            preferred_element_type=jnp.float32,
        )
        for j in range(per)
    ]
    near = jnp.concatenate(sums, axis=0) + jnp.dot(
        fresh_weights, value_ref[...], preferred_element_type=jnp.float32
    )
    out_ref[...] = near / total
    lse_ref[...] = jnp.broadcast_to(peak * SCALE + jnp.log(total), (rows, HD))


def prepare_kernel(*refs):
    prefixes, key_ref, wide_ref = refs[:XS], refs[XS], refs[XS + 1]
    for r, prefix in enumerate(prefixes):
        key_ref[r] = prefix[0]
        wide_ref[r, :, :HD] = prefix[1]
        wide_ref[r, :, HD:] = jnp.ones((prefix.shape[1], HD), jnp.bfloat16)


def far_kernel(group, zs, xs, home_ref, after_ref, query_ref, key_ref, wide_ref, *refs):
    del after_ref
    chunks = len(group)
    outs = refs
    rows = query_ref.shape[1]
    part = rows // xs
    home_z = home_ref[0] // xs
    queries = [query_ref.at[(home_z + (zs - d)) % zs] for d in group]
    line = lax.broadcasted_iota(jnp.int32, (STAT, HD), 0)
    shape = (part, HD)
    diagonal = lax.broadcasted_iota(jnp.int32, shape, 0) == lax.broadcasted_iota(
        jnp.int32, shape, 1
    )
    terms = [jnp.zeros((STAT, HD), jnp.float32)] * chunks
    for r in range(xs):
        query = jnp.concatenate([q[r * part : (r + 1) * part, :] for q in queries], axis=0)
        scores = nt(query, key_ref[r])
        peak = jnp.max(scores, axis=1, keepdims=True)
        weights = jnp.exp2((scores - peak) * (SCALE * LOG2E)).astype(jnp.bfloat16)
        both = jnp.dot(weights, wide_ref[r], preferred_element_type=jnp.float32)
        total = both[:, HD:]
        far = (both[:, :HD] / total).astype(jnp.bfloat16)
        lse = peak * SCALE + jnp.log(total)
        for c in range(chunks):
            outs[c][r * part : (r + 1) * part, :] = far[c * part : (c + 1) * part]
            flat = jnp.sum(
                jnp.where(diagonal, lse[c * part : (c + 1) * part], 0.0), axis=0, keepdims=True
            )
            high = flat.astype(jnp.bfloat16).astype(jnp.float32)
            middle = (flat - high).astype(jnp.bfloat16).astype(jnp.float32)
            low = flat - high - middle
            for k, term in enumerate((high, middle, low)):
                terms[c] = jnp.where(line == k * xs + r, term, terms[c])
    for c in range(chunks):
        outs[c][rows:, :] = terms[c].astype(jnp.bfloat16)


def combine_kernel(xs, home_ref, slot_ref, near_ref, near_lse_ref, *refs):
    chunks, out_ref, far_ref, far_lse_ref = refs[:-3], refs[-3], refs[-2], refs[-1]
    rows = chunks[0].shape[0] - STAT
    part = rows // xs
    home_z = home_ref[0] // xs
    for i, chunk in enumerate(chunks):
        base = pl.multiple_of((home_z + i) % len(chunks) * rows, rows)
        far_ref[pl.ds(base, rows), :] = chunk[:rows, :]
        stats = chunk[rows:, :].astype(jnp.float32)
        stats = stats[:xs] + stats[xs : 2 * xs] + stats[2 * xs : 3 * xs]
        for r in range(xs):
            start = pl.multiple_of(base + r * part, part)
            far_lse_ref[pl.ds(start, part), :] = jnp.broadcast_to(stats[r : r + 1], (part, HD)).T

    def merge(s, _):
        here = pl.ds(pl.multiple_of(s * ROWS, ROWS), ROWS)
        there = pl.ds(pl.multiple_of(slot_ref[s] * ROWS, ROWS), ROWS)
        far = far_ref[there, :].astype(jnp.float32)
        far_lse = far_lse_ref[there, :]
        near_lse = near_lse_ref[here, :]
        peak = jnp.maximum(far_lse, near_lse)
        a = jnp.exp(far_lse - peak)
        b = jnp.exp(near_lse - peak)
        out_ref[here, :] = ((a * far + b * near_ref[here, :]) / (a + b)).astype(jnp.bfloat16)
        return 0

    lax.fori_loop(0, slot_ref.shape[0], merge, 0, unroll=8)


def on_device(queries, new_kv, suffix_cache, prefix_cache, sample_prompt, prefix_slot, suffix_len):
    batch_count = lax.axis_size("batch")
    head_count = lax.axis_size("head")
    own = queries.shape[0]
    samples = suffix_cache.shape[0]
    cap = 2 * samples // batch_count
    block_rows = cap * ROWS
    smem = pl.BlockSpec(memory_space=pltpu.SMEM)
    vmem = pl.BlockSpec(memory_space=pltpu.VMEM)
    anywhere = pl.BlockSpec(memory_space=pl.ANY)
    params = pltpu.CompilerParams(vmem_limit_bytes=VMEM)

    zs = batch_count // XS
    chunk_rows = XS * block_rows

    def along_z(array, d):
        if d == 0:
            return array
        pairs = [
            (z * XS + x, (z + d) % zs * XS + x) for z in range(zs) for x in range(XS)
        ]
        return lax.ppermute(array, "batch", pairs)

    def along_x(array, d):
        pairs = [
            (z * XS + x, z * XS + (x + d) % XS) for z in range(zs) for x in range(XS)
        ]
        return lax.ppermute(array, "batch", pairs)

    home = lax.axis_index("batch").reshape(1)
    own_prefix = prefix_cache[0]
    left = along_x(own_prefix, 1)
    right = along_x(own_prefix, -1)
    opposite = along_x(left, 1)
    prefixes = [own_prefix, right, opposite, left]

    grouped = queries.reshape(own, 2, KVH, GQ, HD).transpose(2, 0, 3, 1, 4)
    grouped = grouped.reshape(head_count, own, ROWS, HD)
    regrouped = lax.all_to_all(grouped, "head", split_axis=0, concat_axis=0, tiled=True)
    regrouped = regrouped.reshape(samples * ROWS, HD)

    slots = pl.pallas_call(
        functools.partial(slots_kernel, cap),
        out_shape=jax.ShapeDtypeStruct((samples,), jnp.int32),
        in_specs=[smem, smem, smem],
        out_specs=smem,
        scratch_shapes=[pltpu.SMEM((batch_count,), jnp.int32)],
        cost_estimate=pl.CostEstimate(flops=1 << 21, bytes_accessed=1 << 20, transcendentals=0),
        name="slots",
    )(home, sample_prompt.reshape(samples), prefix_slot)

    packed = pl.pallas_call(
        pack_kernel,
        out_shape=jax.ShapeDtypeStruct((batch_count * block_rows, HD), jnp.bfloat16),
        in_specs=[smem, vmem, anywhere, anywhere],
        out_specs=vmem,
        compiler_params=params,
        name="pack",
    )(slots, regrouped, left, right)
    rings = [[z * XS + x for z in range(zs)] for x in range(XS)]
    arrived = lax.all_to_all(
        packed.reshape(zs, chunk_rows, HD),
        "batch",
        split_axis=0,
        concat_axis=0,
        tiled=True,
        axis_index_groups=rings,
    )

    per = 16
    fresh_keys = new_kv[:, 0].reshape(2 * samples, HD)
    fresh_values = new_kv[:, 1].reshape(2 * samples, HD)
    cap_len = suffix_cache.shape[2]
    fresh_spec = pl.BlockSpec((HD, HD), lambda i: (i * 2 * per // HD, 0))
    row_spec = pl.BlockSpec((per * ROWS, HD), lambda i: (i, 0))
    near, near_lse = pl.pallas_call(
        functools.partial(near_kernel, per),
        grid=(samples // per,),
        out_shape=[jax.ShapeDtypeStruct((samples * ROWS, HD), jnp.float32)] * 2,
        in_specs=[
            smem,
            row_spec,
            pl.BlockSpec((per, 2, cap_len, HD), lambda i: (i, 0, 0, 0)),
            fresh_spec,
            fresh_spec,
        ],
        out_specs=[row_spec, row_spec],
        compiler_params=params,
        cost_estimate=pl.CostEstimate(flops=1, bytes_accessed=1, transcendentals=0),
        name="near",
    )(suffix_len, regrouped, suffix_cache, fresh_keys, fresh_values)

    prefix_len = prefix_cache.shape[2]
    key_shape = (XS, prefix_len, HD)
    keys, values = pl.pallas_call(
        prepare_kernel,
        out_shape=[
            jax.ShapeDtypeStruct(key_shape, jnp.bfloat16),
            jax.ShapeDtypeStruct((XS, prefix_len, 2 * HD), jnp.bfloat16),
        ],
        in_specs=[vmem] * XS,
        out_specs=[vmem] * 2,
        compiler_params=params,
        cost_estimate=pl.CostEstimate(flops=1, bytes_accessed=1, transcendentals=0),
        name="prepare",
    )(*prefixes)
    groups = [[4], [3, -3], [2, -2], [1, -1], [0]]
    returned = [None] * zs
    after = near_lse
    for group in groups:
        count = len(group)
        outs = pl.pallas_call(
            functools.partial(far_kernel, group, zs, XS),
            out_shape=[jax.ShapeDtypeStruct((chunk_rows + STAT, HD), jnp.bfloat16)] * count,
            in_specs=[smem, anywhere] + [vmem] * 3,
            out_specs=[vmem] * count,
            compiler_params=params,
            cost_estimate=pl.CostEstimate(
                flops=1,
                bytes_accessed=1,
                transcendentals=0,
            ),
            name="far",
        )(home, after, arrived, keys, values)
        after = outs[0]
        if group[0] == 3:
            after = returned[4]
        if group[0] == 2:
            after = returned[3]
        for d, out in zip(group, outs):
            returned[d] = along_z(out, -d)

    result = pl.pallas_call(
        functools.partial(combine_kernel, XS),
        out_shape=jax.ShapeDtypeStruct((samples * ROWS, HD), jnp.bfloat16),
        in_specs=[smem, smem] + [vmem] * (2 + zs),
        out_specs=vmem,
        scratch_shapes=[
            pltpu.VMEM((zs * chunk_rows, HD), jnp.bfloat16),
            pltpu.VMEM((zs * chunk_rows, HD), jnp.float32),
        ],
        compiler_params=params,
        name="combine",
    )(home, slots, near, near_lse, *returned)
    result = result.reshape(head_count, own, ROWS, HD)
    result = lax.all_to_all(result, "head", split_axis=0, concat_axis=0, tiled=True)
    result = result.reshape(head_count, own, GQ, 2, HD).transpose(1, 3, 0, 2, 4)
    return result.reshape(own, 2, QH * HD)


def solution(mesh):
    placed = (
        P(("batch", "head"), None, None),
        P("batch", None, None, "head"),
        P("batch", None, None, "head"),
        P("batch", None, None, "head"),
        P("batch", None),
        P(),
        P("batch"),
    )
    return jax.shard_map(
        on_device,
        mesh=mesh,
        in_specs=placed,
        out_specs=P(("batch", "head"), None, None),
        check_vma=False,
    )
```

profile of v0, /device:TPU:1, one launch (start us, length us, event | category | flops | bytes accessed | tf_op | source)
XLA Modules:
  0.0 110.4 jit_solution(13973872993776492621)
XLA Ops:
  0.0 2.0 %collective-permute-start = (bf16[2,1536,128]{2,1,0:T(8,128)(2,1)}, bf16[2,1536,128]{2,1,0:T(8,128)(2,1)S(1)}, u32[]{:S(2)}, u32[]{:S(2)}) collective-permute-start(bf16[2,1536,128]{2,1,0:T(8,128)(2,1)} %bitcast.19), channel_id=1, source_target_pairs={{0,8},{8,16},{16,24},{24,0},{32,40},{40,48},{48,56},{56,32},{64,72... | collective-permute-start | bytes 2359304 | tf_op jit(solution)/shard_map/ppermute | solution.py:198
  2.0 1.3 %collective-permute-start.1 = (bf16[2,1536,128]{2,1,0:T(8,128)(2,1)}, bf16[2,1536,128]{2,1,0:T(8,128)(2,1)S(1)}, u32[]{:S(2)}, u32[]{:S(2)}) collective-permute-start(bf16[2,1536,128]{2,1,0:T(8,128)(2,1)} %bitcast.20), channel_id=1, source_target_pairs={{0,24},{8,0},{16,8},{24,16},{32,56},{40,32},{48,40},{56,48},{64,88... | collective-permute-start | bytes 2359304 | tf_op jit(solution)/shard_map/ppermute | solution.py:198
  3.3 1.4 %reshape.29 = bf16[16,2,8,8,128]{4,3,2,1,0:T(8,128)(2,1)S(1)} reshape(bf16[16,2,8192]{2,1,0:T(2,128)(2,1)} %param.7) | data formatting | bytes 1048576 | tf_op jit(solution)/shard_map/reshape | solution.py:207
  4.7 1.6 %copy.8 = bf16[8,16,8,2,128]{4,3,2,1,0:T(2,128)(2,1)} copy(bf16[8,16,8,2,128]{4,2,0,3,1:T(8,128)(2,1)S(1)} %bitcast.26) | data formatting | bytes 1048576 | tf_op jit(solution)/shard_map/transpose | solution.py:207
  6.4 6.7 %all-to-all-start = ((bf16[8,16,16,128]{3,2,1,0:T(8,128)(2,1)}), bf16[8,16,16,128]{3,2,1,0:T(8,128)(2,1)S(1)}, u32[]{:S(2)}, u32[]{:S(2)}) async-start(bf16[8,16,16,128]{3,2,1,0:T(8,128)(2,1)} %bitcast.3), calls=%async_computation | async-start | bytes 1048576 | tf_op jit(solution)/shard_map/all_to_all | solution.py:209
  13.1 3.7 %slots.1.slot_ref = s32[128]{0:T(128)} custom-call(s32[1]{0:T(128)} %bitcast.home_ref, s32[128]{0:T(128)} %bitcast.27, s32[32]{0:T(128)} %place_ref.1), custom_call_target="tpu_custom_call" | custom-call | flops 2097152 | bytes 1048576 | tf_op jit(solution)/shard_map/slots/pallas_call | solution.py:212
  16.7 5.8 %all-to-all-done = bf16[8,16,16,128]{3,2,1,0:T(8,128)(2,1)S(1)} async-done(((bf16[8,16,16,128]{3,2,1,0:T(8,128)(2,1)}), bf16[8,16,16,128]{3,2,1,0:T(8,128)(2,1)S(1)}, u32[]{:S(2)}, u32[]{:S(2)}) %all-to-all-start) | async-done | bytes 524320 | tf_op jit(solution)/shard_map/all_to_all | solution.py:209
  23.2 2.1 %pack.1 = bf16[4096,128]{1,0:T(8,128)(2,1)} custom-call(s32[128]{0:T(128)S(1)} %copy-done.8, bf16[2048,128]{1,0:T(8,128)(2,1)S(1)} %bitcast.16, bf16[2,1536,128]{2,1,0:T(8,128)(2,1)S(1)} %collective-permute-done.left_ref.refs_3_, bf16[2,1536,128]{2,1,0:T(8,128)(2,1)S(1)} %collective-permute-done.1.right_ref.refs_1_), custom_call_target="tpu_custom_call" | custom-call | tf_op jit(solution)/shard_map/pack/pallas_call | solution.py:222
  25.3 7.5 %all-to-all-start.1 = ((bf16[8,512,128]{2,1,0:T(8,128)(2,1)}), bf16[8,512,128]{2,1,0:T(8,128)(2,1)S(1)}, u32[]{:S(2)}, u32[]{:S(2)}) async-start(bf16[8,512,128]{2,1,0:T(8,128)(2,1)} %bitcast.8), calls=%async_computation.1 | async-start | bytes 2097152 | tf_op jit(solution)/shard_map/all_to_all | solution.py:231
  32.9 9.3 %near.1 = (f32[2048,128]{1,0:T(8,128)S(1)}, f32[2048,128]{1,0:T(8,128)S(1)}) custom-call(s32[128]{0:T(128)S(1)} %copy-done.10, bf16[2048,128]{1,0:T(8,128)(2,1)S(1)} %bitcast.17, bf16[128,2,128,128]{3,2,1,0:T(8,128)(2,1)} %cache_ref.1, bf16[256,128]{1,0:T(8,128)(2,1)S(1)} %bitcast.23, bf16[256,128]{1,0:T(8,128)(2,1)S(1)} %bitcast.22), custom_call_target="tpu_custom_call" | custom-call | flops 1 | bytes 1 | tf_op jit(solution)/shard_map/near/pallas_call | solution.py:246
  42.3 1.0 copy-done.1
  43.3 1.0 copy-done.5
  44.2 7.6 %collective-permute-done.2.refs_2_ = bf16[2,1536,128]{2,1,0:T(8,128)(2,1)S(1)} collective-permute-done((bf16[2,1536,128]{2,1,0:T(8,128)(2,1)S(1)}, bf16[2,1536,128]{2,1,0:T(8,128)(2,1)S(1)}, u32[]{:S(2)}, u32[]{:S(2)}) %collective-permute-start.2) | collective-permute-done | bytes 786464 | tf_op jit(solution)/shard_map/ppermute | solution.py:198
  51.9 2.2 %prepare.1 = (bf16[4,1536,128]{2,1,0:T(8,128)(2,1)S(1)}, bf16[4,1536,256]{2,1,0:T(8,128)(2,1)}) custom-call(bf16[2,1536,128]{2,1,0:T(8,128)(2,1)S(1)} %bitcast.21, bf16[2,1536,128]{2,1,0:T(8,128)(2,1)S(1)} %copy-done.4, bf16[2,1536,128]{2,1,0:T(8,128)(2,1)S(1)} %collective-permute-done.2.refs_2_, bf16[2,1536,128]{2,1,0:T(8,128)(2,1)S(1)} %collective-permute-done.left_ref.refs_3_), custom_call_target="tpu_custom_call" | custom-call | flops 1 | bytes 1 | tf_op jit(solution)/shard_map/prepare/pallas_call | solution.py:265
  54.1 7.9 %all-to-all-done.1.query_ref = bf16[8,512,128]{2,1,0:T(8,128)(2,1)S(1)} async-done(((bf16[8,512,128]{2,1,0:T(8,128)(2,1)}), bf16[8,512,128]{2,1,0:T(8,128)(2,1)S(1)}, u32[]{:S(2)}, u32[]{:S(2)}) %all-to-all-start.1) | async-done | bytes 1048608 | tf_op jit(solution)/shard_map/all_to_all | solution.py:231
  61.9 1.2 %copy-done.2 = f32[2048,128]{1,0:T(8,128)S(1)} copy-done((f32[2048,128]{1,0:T(8,128)S(1)}, f32[2048,128]{1,0:T(8,128)}, u32[]{:S(2)}) %copy-start.2) | copy-done | bytes 1048600
  63.2 3.5 %far.5.after_ref = bf16[528,128]{1,0:T(8,128)(2,1)S(1)} custom-call(s32[1]{0:T(128)} %bitcast.home_ref, f32[2048,128]{1,0:T(8,128)S(1)} %copy-done.2, bf16[8,512,128]{2,1,0:T(8,128)(2,1)S(1)} %all-to-all-done.1.query_ref, bf16[4,1536,128]{2,1,0:T(8,128)(2,1)S(1)} %get-tuple-element.17.key_ref, bf16[4,1536,256]{2,1,0:T(8,128)(2,1)} %get-tuple-element.18.wide_ref), custom_call_target="tpu_custom_call" | custom-call | flops 1 | bytes 1 | tf_op jit(solution)/shard_map/far/pallas_call | solution.py:282
  66.8 2.5 %far.6 = (bf16[528,128]{1,0:T(8,128)(2,1)S(1)}, bf16[528,128]{1,0:T(8,128)(2,1)S(1)}) custom-call(s32[1]{0:T(128)} %bitcast.home_ref, bf16[528,128]{1,0:T(8,128)(2,1)S(1)} %far.5.after_ref, bf16[8,512,128]{2,1,0:T(8,128)(2,1)S(1)} %all-to-all-done.1.query_ref, bf16[4,1536,128]{2,1,0:T(8,128)(2,1)S(1)} %get-tuple-element.17.key_ref, ...), custom_call_target="tpu_custom_call" | custom-call | flops 1 | bytes 1 | tf_op jit(solution)/shard_map/far/pallas_call | solution.py:282
  69.2 1.3 %collective-permute-start.3 = (bf16[528,128]{1,0:T(8,128)(2,1)S(1)}, bf16[528,128]{1,0:T(8,128)(2,1)S(1)}, u32[]{:S(2)}, u32[]{:S(2)}) collective-permute-start(bf16[528,128]{1,0:T(8,128)(2,1)S(1)} %get-tuple-element.19), channel_id=1, source_target_pairs={{0,160},{8,168},{16,176},{24,184},{32,192},{40,200},{48,208},{56,2... | collective-permute-start | bytes 405512 | tf_op jit(solution)/shard_map/ppermute | solution.py:192
  70.6 2.0 %collective-permute-start.7 = (bf16[528,128]{1,0:T(8,128)(2,1)S(1)}, bf16[528,128]{1,0:T(8,128)(2,1)S(1)}, u32[]{:S(2)}, u32[]{:S(2)}) collective-permute-start(bf16[528,128]{1,0:T(8,128)(2,1)S(1)} %get-tuple-element.22), channel_id=1, source_target_pairs={{0,96},{8,104},{16,112},{24,120},{32,128},{40,136},{48,144},{56,15... | collective-permute-start | bytes 405512 | tf_op jit(solution)/shard_map/ppermute | solution.py:192
  72.6 4.6 %collective-permute-done.5.after_ref.refs_4_ = bf16[528,128]{1,0:T(8,128)(2,1)S(1)} collective-permute-done((bf16[528,128]{1,0:T(8,128)(2,1)S(1)}, bf16[528,128]{1,0:T(8,128)(2,1)S(1)}, u32[]{:S(2)}, u32[]{:S(2)}) %collective-permute-start.5) | collective-permute-done | bytes 135200 | tf_op jit(solution)/shard_map/ppermute | solution.py:192
  77.2 2.5 %far.9 = (bf16[528,128]{1,0:T(8,128)(2,1)S(1)}, bf16[528,128]{1,0:T(8,128)(2,1)S(1)}) custom-call(s32[1]{0:T(128)} %bitcast.home_ref, bf16[528,128]{1,0:T(8,128)(2,1)S(1)} %collective-permute-done.5.after_ref.refs_4_, bf16[8,512,128]{2,1,0:T(8,128)(2,1)S(1)} %all-to-all-done.1.query_ref, bf16[4,1536,128]{2,1,0:T(8,128)(2,1)S(1)} %get-tuple-element.17.key_ref, ...), custom_call_target="tpu_custom_call" | custom-call | flops 1 | bytes 1 | tf_op jit(solution)/shard_map/far/pallas_call | solution.py:282
  80.5 1.6 %collective-permute-start.8 = (bf16[528,128]{1,0:T(8,128)(2,1)S(1)}, bf16[528,128]{1,0:T(8,128)(2,1)S(1)}, u32[]{:S(2)}, u32[]{:S(2)}) collective-permute-start(bf16[528,128]{1,0:T(8,128)(2,1)S(1)} %get-tuple-element.23), channel_id=1, source_target_pairs={{0,64},{8,72},{16,80},{24,88},{32,96},{40,104},{48,112},{56,120},{... | collective-permute-start | bytes 405512 | tf_op jit(solution)/shard_map/ppermute | solution.py:192
  82.1 2.5 %far.7 = (bf16[528,128]{1,0:T(8,128)(2,1)S(1)}, bf16[528,128]{1,0:T(8,128)(2,1)S(1)}) custom-call(s32[1]{0:T(128)} %bitcast.home_ref, bf16[528,128]{1,0:T(8,128)(2,1)S(1)} %collective-permute-done.3.after_ref.refs_3_, bf16[8,512,128]{2,1,0:T(8,128)(2,1)S(1)} %all-to-all-done.1.query_ref, bf16[4,1536,128]{2,1,0:T(8,128)(2,1)S(1)} %get-tuple-element.17.key_ref, ...), custom_call_target="tpu_custom_call" | custom-call | flops 1 | bytes 1 | tf_op jit(solution)/shard_map/far/pallas_call | solution.py:282
  84.6 0.9 collective-permute-start.4
  85.5 3.4 %collective-permute-start.9 = (bf16[528,128]{1,0:T(8,128)(2,1)S(1)}, bf16[528,128]{1,0:T(8,128)(2,1)S(1)}, u32[]{:S(2)}, u32[]{:S(2)}) collective-permute-start(bf16[528,128]{1,0:T(8,128)(2,1)S(1)} %get-tuple-element.24), channel_id=1, source_target_pairs={{0,32},{8,40},{16,48},{24,56},{32,64},{40,72},{48,80},{56,88},{64,... | collective-permute-start | bytes 405512 | tf_op jit(solution)/shard_map/ppermute | solution.py:192
  89.0 1.4 %far.8.refs_0_ = bf16[528,128]{1,0:T(8,128)(2,1)S(1)} custom-call(s32[1]{0:T(128)} %bitcast.home_ref, bf16[528,128]{1,0:T(8,128)(2,1)S(1)} %get-tuple-element.20.after_ref, bf16[8,512,128]{2,1,0:T(8,128)(2,1)S(1)} %all-to-all-done.1.query_ref, bf16[4,1536,128]{2,1,0:T(8,128)(2,1)S(1)} %get-tuple-element.17.key_ref, bf16[4,1536,256]{2,1,0:T(8,128)(2,1)S(1)} %copy-done), custom_call_target="tpu_custom_call" | custom-call | flops 1 | bytes 1 | tf_op jit(solution)/shard_map/far/pallas_call | solution.py:282
  90.4 1.1 collective-permute-done.8.refs_6_
  91.5 1.3 %collective-permute-done.4.refs_1_ = bf16[528,128]{1,0:T(8,128)(2,1)S(1)} collective-permute-done((bf16[528,128]{1,0:T(8,128)(2,1)S(1)}, bf16[528,128]{1,0:T(8,128)(2,1)S(1)}, u32[]{:S(2)}, u32[]{:S(2)}) %collective-permute-start.4) | collective-permute-done | bytes 135200 | tf_op jit(solution)/shard_map/ppermute | solution.py:192
  92.8 1.0 collective-permute-done.9.refs_7_
  93.8 2.0 %combine.1 = bf16[2048,128]{1,0:T(8,128)(2,1)S(1)} custom-call(s32[1]{0:T(128)} %bitcast.home_ref, s32[128]{0:T(128)S(1)} %copy-done.9, f32[2048,128]{1,0:T(8,128)S(1)} %copy-done.6, f32[2048,128]{1,0:T(8,128)S(1)} %copy-done.2, bf16[528,128]{1,0:T(8,128)(2,1)S(1)} %far.8.refs_0_, bf16[528,128]{1,0:T(8,128)(2,1)S(1)} %collective-permute-done.4.refs_1_, ...), custom_call_target="tpu_custom_call" | custom-call | tf_op jit(solution)/shard_map/combine/pallas_call | solution.py:303
  95.8 13.5 %all_to_all.15 = bf16[8,16,16,128]{3,2,1,0:T(8,128)(2,1)S(1)} all-to-all(bf16[8,16,16,128]{3,2,1,0:T(8,128)(2,1)S(1)} %bitcast.18), channel_id=1, replica_groups=mesh['batch'=32,'head'=8] {'head'}, dimensions={0} | all-to-all | bytes 1048576 | tf_op jit(solution)/shard_map/all_to_all | solution.py:316
  (32 shorter events, 2.8 us)
Async XLA Ops:
  0.0 22.6 %collective-permute-start = (bf16[2,1536,128]{2,1,0:T(8,128)(2,1)}, bf16[2,1536,128]{2,1,0:T(8,128)(2,1)S(1)}, u32[]{:S(2)}, u32[]{:S(2)}) collective-permute-start(bf16[2,1536,128]{2,1,0:T(8,128)(2,1)} %bitcast.19), channel_id=1, source_target_pairs={{0,8},{8,16},{16,24},{24,0},{32,40},{40,48},{48,56},{56,32},{64,72... | collective-permute-start | bytes 2359304 | tf_op jit(solution)/shard_map/ppermute | solution.py:198
  2.0 20.5 %collective-permute-start.1 = (bf16[2,1536,128]{2,1,0:T(8,128)(2,1)}, bf16[2,1536,128]{2,1,0:T(8,128)(2,1)S(1)}, u32[]{:S(2)}, u32[]{:S(2)}) collective-permute-start(bf16[2,1536,128]{2,1,0:T(8,128)(2,1)} %bitcast.20), channel_id=1, source_target_pairs={{0,24},{8,0},{16,8},{24,16},{32,56},{40,32},{48,40},{56,48},{64,88... | collective-permute-start | bytes 2359304 | tf_op jit(solution)/shard_map/ppermute | solution.py:198
  6.4 26.4 %copy-start.11 = (bf16[128,2,2,128]{3,2,1,0:T(2,128)(2,1)S(1)}, bf16[128,2,2,128]{3,2,1,0:T(2,128)(2,1)}, u32[]{:S(2)}) copy-start(bf16[128,2,2,128]{3,2,1,0:T(2,128)(2,1)} %param.8) | copy-start | bytes 393220
  6.4 26.5 %copy-start.10 = (s32[128]{0:T(128)S(1)}, s32[128]{0:T(128)}, u32[]{:S(2)}) copy-start(s32[128]{0:T(128)} %len_ref.1) | copy-start | bytes 1540
  6.4 16.2 %all-to-all-start = ((bf16[8,16,16,128]{3,2,1,0:T(8,128)(2,1)}), bf16[8,16,16,128]{3,2,1,0:T(8,128)(2,1)S(1)}, u32[]{:S(2)}, u32[]{:S(2)}) async-start(bf16[8,16,16,128]{3,2,1,0:T(8,128)(2,1)} %bitcast.3), calls=%async_computation | async-start | bytes 1048576 | tf_op jit(solution)/shard_map/all_to_all | solution.py:209
  22.6 10.3 %copy-start.3 = (bf16[2,1536,128]{2,1,0:T(8,128)(2,1)}, bf16[2,1536,128]{2,1,0:T(8,128)(2,1)S(1)}, u32[]{:S(2)}) copy-start(bf16[2,1536,128]{2,1,0:T(8,128)(2,1)S(1)} %collective-permute-done.1.right_ref.refs_1_) | copy-start | bytes 2359300
  22.6 0.6 copy-start.8
  25.3 36.7 %all-to-all-start.1 = ((bf16[8,512,128]{2,1,0:T(8,128)(2,1)}), bf16[8,512,128]{2,1,0:T(8,128)(2,1)S(1)}, u32[]{:S(2)}, u32[]{:S(2)}) async-start(bf16[8,512,128]{2,1,0:T(8,128)(2,1)} %bitcast.8), calls=%async_computation.1 | async-start | bytes 2097152 | tf_op jit(solution)/shard_map/all_to_all | solution.py:231
  32.8 19.1 %collective-permute-start.2 = (bf16[2,1536,128]{2,1,0:T(8,128)(2,1)S(1)}, bf16[2,1536,128]{2,1,0:T(8,128)(2,1)S(1)}, u32[]{:S(2)}, u32[]{:S(2)}) collective-permute-start(bf16[2,1536,128]{2,1,0:T(8,128)(2,1)S(1)} %collective-permute-done.left_ref.refs_3_), channel_id=1, source_target_pairs={{0,8},{8,16},{16,24},{24,0},{32,40},{40,48},{48,56},{56,32},{64,72... | collective-permute-start | bytes 2359304 | tf_op jit(solution)/shard_map/ppermute | solution.py:198
  32.9 19.0 %copy-start.4 = (bf16[2,1536,128]{2,1,0:T(8,128)(2,1)S(1)}, bf16[2,1536,128]{2,1,0:T(8,128)(2,1)}, u32[]{:S(2)}) copy-start(bf16[2,1536,128]{2,1,0:T(8,128)(2,1)} %copy-done.3) | copy-start | bytes 2359300
  32.9 18.9 %copy-start.7 = (bf16[1,2,1536,128]{3,2,1,0:T(8,128)(2,1)S(1)}, bf16[1,2,1536,128]{3,2,1,0:T(8,128)(2,1)}, u32[]{:S(2)}) copy-start(bf16[1,2,1536,128]{3,2,1,0:T(8,128)(2,1)} %param.10) | copy-start | bytes 2359300
  42.2 1.0 copy-start.1
  43.3 1.0 copy-start.5
  61.9 1.2 %copy-start.2 = (f32[2048,128]{1,0:T(8,128)S(1)}, f32[2048,128]{1,0:T(8,128)}, u32[]{:S(2)}) copy-start(f32[2048,128]{1,0:T(8,128)} %copy-done.1) | copy-start | bytes 3145732
  63.2 3.6 %copy-start = (bf16[4,1536,256]{2,1,0:T(8,128)(2,1)S(1)}, bf16[4,1536,256]{2,1,0:T(8,128)(2,1)}, u32[]{:S(2)}) copy-start(bf16[4,1536,256]{2,1,0:T(8,128)(2,1)} %get-tuple-element.18.wide_ref) | copy-start | bytes 9437188
  66.7 10.5 %collective-permute-start.5 = (bf16[528,128]{1,0:T(8,128)(2,1)S(1)}, bf16[528,128]{1,0:T(8,128)(2,1)S(1)}, u32[]{:S(2)}, u32[]{:S(2)}) collective-permute-start(bf16[528,128]{1,0:T(8,128)(2,1)S(1)} %far.5.after_ref), channel_id=1, source_target_pairs={{0,128},{8,136},{16,144},{24,152},{32,160},{40,168},{48,176},{56,1... | collective-permute-start | bytes 405512 | tf_op jit(solution)/shard_map/ppermute | solution.py:192
  69.2 12.9 %collective-permute-start.3 = (bf16[528,128]{1,0:T(8,128)(2,1)S(1)}, bf16[528,128]{1,0:T(8,128)(2,1)S(1)}, u32[]{:S(2)}, u32[]{:S(2)}) collective-permute-start(bf16[528,128]{1,0:T(8,128)(2,1)S(1)} %get-tuple-element.19), channel_id=1, source_target_pairs={{0,160},{8,168},{16,176},{24,184},{32,192},{40,200},{48,208},{56,2... | collective-permute-start | bytes 405512 | tf_op jit(solution)/shard_map/ppermute | solution.py:192
  70.6 19.8 %collective-permute-start.7 = (bf16[528,128]{1,0:T(8,128)(2,1)S(1)}, bf16[528,128]{1,0:T(8,128)(2,1)S(1)}, u32[]{:S(2)}, u32[]{:S(2)}) collective-permute-start(bf16[528,128]{1,0:T(8,128)(2,1)S(1)} %get-tuple-element.22), channel_id=1, source_target_pairs={{0,96},{8,104},{16,112},{24,120},{32,128},{40,136},{48,144},{56,15... | collective-permute-start | bytes 405512 | tf_op jit(solution)/shard_map/ppermute | solution.py:192
  79.7 10.8 %collective-permute-start.6 = (bf16[528,128]{1,0:T(8,128)(2,1)S(1)}, bf16[528,128]{1,0:T(8,128)(2,1)S(1)}, u32[]{:S(2)}, u32[]{:S(2)}) collective-permute-start(bf16[528,128]{1,0:T(8,128)(2,1)S(1)} %get-tuple-element.21), channel_id=1, source_target_pairs={{0,192},{8,200},{16,208},{24,216},{32,224},{40,232},{48,240},{56,2... | collective-permute-start | bytes 405512 | tf_op jit(solution)/shard_map/ppermute | solution.py:192
  80.5 10.9 %collective-permute-start.8 = (bf16[528,128]{1,0:T(8,128)(2,1)S(1)}, bf16[528,128]{1,0:T(8,128)(2,1)S(1)}, u32[]{:S(2)}, u32[]{:S(2)}) collective-permute-start(bf16[528,128]{1,0:T(8,128)(2,1)S(1)} %get-tuple-element.23), channel_id=1, source_target_pairs={{0,64},{8,72},{16,80},{24,88},{32,96},{40,104},{48,112},{56,120},{... | collective-permute-start | bytes 405512 | tf_op jit(solution)/shard_map/ppermute | solution.py:192
  84.6 9.2 %copy-start.6 = (f32[2048,128]{1,0:T(8,128)S(1)}, f32[2048,128]{1,0:T(8,128)}, u32[]{:S(2)}) copy-start(f32[2048,128]{1,0:T(8,128)} %copy-done.5) | copy-start | bytes 3145732
  84.6 9.2 %copy-start.9 = (s32[128]{0:T(128)S(1)}, s32[128]{0:T(128)}, u32[]{:S(2)}) copy-start(s32[128]{0:T(128)} %slots.1.slot_ref) | copy-start | bytes 1540
  84.6 8.2 %collective-permute-start.4 = (bf16[528,128]{1,0:T(8,128)(2,1)S(1)}, bf16[528,128]{1,0:T(8,128)(2,1)S(1)}, u32[]{:S(2)}, u32[]{:S(2)}) collective-permute-start(bf16[528,128]{1,0:T(8,128)(2,1)S(1)} %get-tuple-element.20.after_ref), channel_id=1, source_target_pairs={{0,224},{8,232},{16,240},{24,248},{32,0},{40,8},{48,16},{56,24},{6... | collective-permute-start | bytes 405512 | tf_op jit(solution)/shard_map/ppermute | solution.py:192
  85.5 8.3 %collective-permute-start.9 = (bf16[528,128]{1,0:T(8,128)(2,1)S(1)}, bf16[528,128]{1,0:T(8,128)(2,1)S(1)}, u32[]{:S(2)}, u32[]{:S(2)}) collective-permute-start(bf16[528,128]{1,0:T(8,128)(2,1)S(1)} %get-tuple-element.24), channel_id=1, source_target_pairs={{0,32},{8,40},{16,48},{24,56},{32,64},{40,72},{48,80},{56,88},{64,... | collective-permute-start | bytes 405512 | tf_op jit(solution)/shard_map/ppermute | solution.py:192
where the time goes:
time: 111 us; the launch traced here: 110 us
  Pallas kernels  31.6 us (28%)
  waiting for transfers between devices  29.3 us (26%)
  starting transfers between devices  27.7 us (25%)
  blocking collectives  13.5 us (12%)
  local copies, waits for them, and re-layouts  7.99 us (7%)
    all_to_all x1, blocking collectives, on_device(): lax.all_to_all(result, 'head', split_axis=0, concat_axis=0, tiled=True)  13.5 us
    pallas_call x5, Pallas kernels, on_device(): pl.pallas_call(functools.partial(far_kernel, group, zs, XS), out_shape=[j...  12.3 us
    ppermute x7, starting transfers between devices, along_z(): return lax.ppermute(array, 'batch', pairs)  10.2 us
    pallas_call x1, Pallas kernels, on_device(): pl.pallas_call(functools.partial(near_kernel, per), grid=(samples // per,...  9.32 us
    ppermute x7, waiting for transfers between devices, along_z(): return lax.ppermute(array, 'batch', pairs)  7.98 us
    all_to_all x1, waiting for transfers between devices, on_device(): lax.all_to_all(packed.reshape(zs, chunk_rows, HD), 'batch', split_axis=0,...  7.89 us
    ppermute x3, waiting for transfers between devices, along_x(): return lax.ppermute(array, 'batch', pairs)  7.63 us
    all_to_all x1, starting transfers between devices, on_device(): lax.all_to_all(packed.reshape(zs, chunk_rows, HD), 'batch', split_axis=0,...  7.5 us
  transfers between devices with their start and end apart: 12, of which 7 were waited for; matrix products, arithmetic and copies ran while one was open for 3% of the time, Pallas kernels for 22%

commit v1 on v0

--- a/solution.py
+++ b/solution.py
@@ -21,6 +21,26 @@
 
 def nt(a, b):
     return lax.dot_general(a, b, (((1,), (1,)), ((), ())), preferred_element_type=jnp.float32)
+
+
+def split_kernel(query_hbm, out_ref, query_ref, sems):
+    parts = sems.shape[0]
+    size = query_ref.shape[0] // parts
+    copies = []
+    for p in range(parts):
+        rows = pl.ds(p * size, size)
+        copies.append(
+            pltpu.make_async_copy(query_hbm.at[rows], query_ref.at[rows], sems.at[p])
+        )
+    for copy in copies:
+        copy.start()
+    for p in range(parts):
+        copies[p].wait()
+        rows = pl.ds(p * size, size)
+        for g in range(out_ref.shape[0]):
+            for r in range(GQ):
+                lanes = pl.ds((g * GQ + r) * HD, HD)
+                out_ref[g, rows, 2 * r : 2 * r + 2, :] = query_ref[rows, :, lanes]
 
 
 def slots_kernel(cap, home_ref, prompt_ref, place_ref, slot_ref, count_ref):
@@ -204,8 +224,16 @@
     opposite = along_x(left, 1)
     prefixes = [own_prefix, right, opposite, left]
 
-    grouped = queries.reshape(own, 2, KVH, GQ, HD).transpose(2, 0, 3, 1, 4)
-    grouped = grouped.reshape(head_count, own, ROWS, HD)
+    parts = 2
+    grouped = pl.pallas_call(
+        split_kernel,
+        out_shape=jax.ShapeDtypeStruct((head_count, own, ROWS, HD), jnp.bfloat16),
+        in_specs=[anywhere],
+        out_specs=vmem,
+        scratch_shapes=[pltpu.VMEM(queries.shape, jnp.bfloat16), pltpu.SemaphoreType.DMA((parts,))],
+        compiler_params=params,
+        name="split",
+    )(queries)
     regrouped = lax.all_to_all(grouped, "head", split_axis=0, concat_axis=0, tiled=True)
     regrouped = regrouped.reshape(samples * ROWS, HD)
 

time: 111 us -> 111 us (level)
  local copies, waits for them, and re-layouts: 7.99 us -> 6.07 us
  Pallas kernels: 31.6 us -> 33.1 us
    transpose x1 -> x0, local copies, waits for them, and re-layouts: 1.6 us -> none  [on_device(): grouped = queries.reshape(own, 2, KVH, GQ, HD).transpose(2, 0, 3, 1, 4)]
    pallas_call x0 -> x1, Pallas kernels: none -> 1.53 us  [on_device(): pl.pallas_call(split_kernel, out_shape=jax.ShapeDtypeStruct((head_count,...]
    reshape x1 -> x0, local copies, waits for them, and re-layouts: 1.43 us -> none  [on_device(): grouped = queries.reshape(own, 2, KVH, GQ, HD).transpose(2, 0, 3, 1, 4)]
    unnamed x24 -> x26, local copies, waits for them, and re-layouts: 3.82 us -> 4.94 us
  transfers between devices with their start and end apart: 12 -> 12, of which waited for: 7 -> 7; matrix products, arithmetic and copies ran while one was open for 3% -> 0% of each run, Pallas kernels for 22% -> 23%
where the time goes in v1:
time: 111 us; the launch traced here: 110 us
  Pallas kernels  33.1 us (30%)
  waiting for transfers between devices  29.2 us (26%)
  starting transfers between devices  27.9 us (25%)
  blocking collectives  14 us (13%)
  local copies, waits for them, and re-layouts  6.07 us (5%)
    all_to_all x1, blocking collectives, on_device(): lax.all_to_all(result, 'head', split_axis=0, concat_axis=0, tiled=True)  14 us
    pallas_call x5, Pallas kernels, on_device(): pl.pallas_call(functools.partial(far_kernel, group, zs, XS), out_shape=[j...  12.3 us
    ppermute x7, starting transfers between devices, along_z(): return lax.ppermute(array, 'batch', pairs)  10.2 us
    pallas_call x1, Pallas kernels, on_device(): pl.pallas_call(functools.partial(near_kernel, per), grid=(samples // per,...  9.32 us
    ppermute x7, waiting for transfers between devices, along_z(): return lax.ppermute(array, 'batch', pairs)  7.98 us
    all_to_all x1, waiting for transfers between devices, on_device(): lax.all_to_all(packed.reshape(zs, chunk_rows, HD), 'batch', split_axis=0,...  7.89 us
    ppermute x3, waiting for transfers between devices, along_x(): return lax.ppermute(array, 'batch', pairs)  7.53 us
    all_to_all x1, starting transfers between devices, on_device(): lax.all_to_all(packed.reshape(zs, chunk_rows, HD), 'batch', split_axis=0,...  7.5 us
  transfers between devices with their start and end apart: 12, of which 7 were waited for; matrix products, arithmetic and copies ran while one was open for 0% of the time, Pallas kernels for 23%

profile of v1, /device:TPU:1, one launch (start us, length us, event | category | flops | bytes accessed | tf_op | source)
XLA Modules:
  0.0 110.4 jit_solution(10199368760169489003)
XLA Ops:
  0.0 2.0 %collective-permute-start = (bf16[2,1536,128]{2,1,0:T(8,128)(2,1)}, bf16[2,1536,128]{2,1,0:T(8,128)(2,1)S(1)}, u32[]{:S(2)}, u32[]{:S(2)}) collective-permute-start(bf16[2,1536,128]{2,1,0:T(8,128)(2,1)} %bitcast.17), channel_id=1, source_target_pairs={{0,8},{8,16},{16,24},{24,0},{32,40},{40,48},{48,56},{56,32},{64,72... | collective-permute-start | bytes 2359304 | tf_op jit(solution)/shard_map/ppermute | solution.py:218
  2.0 1.3 %collective-permute-start.1 = (bf16[2,1536,128]{2,1,0:T(8,128)(2,1)}, bf16[2,1536,128]{2,1,0:T(8,128)(2,1)S(1)}, u32[]{:S(2)}, u32[]{:S(2)}) collective-permute-start(bf16[2,1536,128]{2,1,0:T(8,128)(2,1)} %bitcast.18), channel_id=1, source_target_pairs={{0,24},{8,0},{16,8},{24,16},{32,56},{40,32},{48,40},{56,48},{64,88... | collective-permute-start | bytes 2359304 | tf_op jit(solution)/shard_map/ppermute | solution.py:218
  3.3 1.0 copy-done.8
  4.4 1.5 %split.1 = bf16[8,16,16,128]{3,2,1,0:T(8,128)(2,1)} custom-call(bf16[16,2,8192]{2,1,0:T(2,128)(2,1)S(1)} %copy-done.8), custom_call_target="tpu_custom_call" | custom-call | tf_op jit(solution)/shard_map/split/pallas_call | solution.py:228
  5.9 6.7 %all-to-all-start = ((bf16[8,16,16,128]{3,2,1,0:T(8,128)(2,1)}), bf16[8,16,16,128]{3,2,1,0:T(8,128)(2,1)S(1)}, u32[]{:S(2)}, u32[]{:S(2)}) async-start(bf16[8,16,16,128]{3,2,1,0:T(8,128)(2,1)} %split.1), calls=%async_computation | async-start | bytes 1048576 | tf_op jit(solution)/shard_map/all_to_all | solution.py:237
  12.6 3.7 %slots.1.slot_ref = s32[128]{0:T(128)} custom-call(s32[1]{0:T(128)} %bitcast.home_ref, s32[128]{0:T(128)} %bitcast.24, s32[32]{0:T(128)} %place_ref.1), custom_call_target="tpu_custom_call" | custom-call | flops 2097152 | bytes 1048576 | tf_op jit(solution)/shard_map/slots/pallas_call | solution.py:240
  16.3 5.8 %all-to-all-done = bf16[8,16,16,128]{3,2,1,0:T(8,128)(2,1)S(1)} async-done(((bf16[8,16,16,128]{3,2,1,0:T(8,128)(2,1)}), bf16[8,16,16,128]{3,2,1,0:T(8,128)(2,1)S(1)}, u32[]{:S(2)}, u32[]{:S(2)}) %all-to-all-start) | async-done | bytes 524320 | tf_op jit(solution)/shard_map/all_to_all | solution.py:237
  22.8 2.1 %pack.1 = bf16[4096,128]{1,0:T(8,128)(2,1)} custom-call(s32[128]{0:T(128)S(1)} %copy-done.9, bf16[2048,128]{1,0:T(8,128)(2,1)S(1)} %bitcast.14, bf16[2,1536,128]{2,1,0:T(8,128)(2,1)S(1)} %collective-permute-done.left_ref.refs_3_, bf16[2,1536,128]{2,1,0:T(8,128)(2,1)S(1)} %collective-permute-done.1.right_ref.refs_1_), custom_call_target="tpu_custom_call" | custom-call | tf_op jit(solution)/shard_map/pack/pallas_call | solution.py:250
  24.9 7.5 %all-to-all-start.1 = ((bf16[8,512,128]{2,1,0:T(8,128)(2,1)}), bf16[8,512,128]{2,1,0:T(8,128)(2,1)S(1)}, u32[]{:S(2)}, u32[]{:S(2)}) async-start(bf16[8,512,128]{2,1,0:T(8,128)(2,1)} %bitcast.6), calls=%async_computation.1 | async-start | bytes 2097152 | tf_op jit(solution)/shard_map/all_to_all | solution.py:259
  32.6 9.3 %near.1 = (f32[2048,128]{1,0:T(8,128)S(1)}, f32[2048,128]{1,0:T(8,128)S(1)}) custom-call(s32[128]{0:T(128)S(1)} %copy-done.11, bf16[2048,128]{1,0:T(8,128)(2,1)S(1)} %bitcast.15, bf16[128,2,128,128]{3,2,1,0:T(8,128)(2,1)} %cache_ref.1, bf16[256,128]{1,0:T(8,128)(2,1)S(1)} %bitcast.21, bf16[256,128]{1,0:T(8,128)(2,1)S(1)} %bitcast.20), custom_call_target="tpu_custom_call" | custom-call | flops 1 | bytes 1 | tf_op jit(solution)/shard_map/near/pallas_call | solution.py:274
  42.0 1.0 copy-done.1
  43.0 1.0 copy-done.5
  43.9 7.5 %collective-permute-done.2.refs_2_ = bf16[2,1536,128]{2,1,0:T(8,128)(2,1)S(1)} collective-permute-done((bf16[2,1536,128]{2,1,0:T(8,128)(2,1)S(1)}, bf16[2,1536,128]{2,1,0:T(8,128)(2,1)S(1)}, u32[]{:S(2)}, u32[]{:S(2)}) %collective-permute-start.2) | collective-permute-done | bytes 786464 | tf_op jit(solution)/shard_map/ppermute | solution.py:218
  51.5 2.2 %prepare.1 = (bf16[4,1536,128]{2,1,0:T(8,128)(2,1)S(1)}, bf16[4,1536,256]{2,1,0:T(8,128)(2,1)}) custom-call(bf16[2,1536,128]{2,1,0:T(8,128)(2,1)S(1)} %bitcast.19, bf16[2,1536,128]{2,1,0:T(8,128)(2,1)S(1)} %copy-done.4, bf16[2,1536,128]{2,1,0:T(8,128)(2,1)S(1)} %collective-permute-done.2.refs_2_, bf16[2,1536,128]{2,1,0:T(8,128)(2,1)S(1)} %collective-permute-done.left_ref.refs_3_), custom_call_target="tpu_custom_call" | custom-call | flops 1 | bytes 1 | tf_op jit(solution)/shard_map/prepare/pallas_call | solution.py:293
  53.7 7.9 %all-to-all-done.1.query_ref = bf16[8,512,128]{2,1,0:T(8,128)(2,1)S(1)} async-done(((bf16[8,512,128]{2,1,0:T(8,128)(2,1)}), bf16[8,512,128]{2,1,0:T(8,128)(2,1)S(1)}, u32[]{:S(2)}, u32[]{:S(2)}) %all-to-all-start.1) | async-done | bytes 1048608 | tf_op jit(solution)/shard_map/all_to_all | solution.py:259
  61.6 1.2 %copy-done.2 = f32[2048,128]{1,0:T(8,128)S(1)} copy-done((f32[2048,128]{1,0:T(8,128)S(1)}, f32[2048,128]{1,0:T(8,128)}, u32[]{:S(2)}) %copy-start.2) | copy-done | bytes 1048600
  62.8 3.5 %far.5.after_ref = bf16[528,128]{1,0:T(8,128)(2,1)S(1)} custom-call(s32[1]{0:T(128)} %bitcast.home_ref, f32[2048,128]{1,0:T(8,128)S(1)} %copy-done.2, bf16[8,512,128]{2,1,0:T(8,128)(2,1)S(1)} %all-to-all-done.1.query_ref, bf16[4,1536,128]{2,1,0:T(8,128)(2,1)S(1)} %get-tuple-element.17.key_ref, bf16[4,1536,256]{2,1,0:T(8,128)(2,1)} %get-tuple-element.18.wide_ref), custom_call_target="tpu_custom_call" | custom-call | flops 1 | bytes 1 | tf_op jit(solution)/shard_map/far/pallas_call | solution.py:310
  66.4 2.5 %far.6 = (bf16[528,128]{1,0:T(8,128)(2,1)S(1)}, bf16[528,128]{1,0:T(8,128)(2,1)S(1)}) custom-call(s32[1]{0:T(128)} %bitcast.home_ref, bf16[528,128]{1,0:T(8,128)(2,1)S(1)} %far.5.after_ref, bf16[8,512,128]{2,1,0:T(8,128)(2,1)S(1)} %all-to-all-done.1.query_ref, bf16[4,1536,128]{2,1,0:T(8,128)(2,1)S(1)} %get-tuple-element.17.key_ref, ...), custom_call_target="tpu_custom_call" | custom-call | flops 1 | bytes 1 | tf_op jit(solution)/shard_map/far/pallas_call | solution.py:310
  68.9 1.3 %collective-permute-start.3 = (bf16[528,128]{1,0:T(8,128)(2,1)S(1)}, bf16[528,128]{1,0:T(8,128)(2,1)S(1)}, u32[]{:S(2)}, u32[]{:S(2)}) collective-permute-start(bf16[528,128]{1,0:T(8,128)(2,1)S(1)} %get-tuple-element.19), channel_id=1, source_target_pairs={{0,160},{8,168},{16,176},{24,184},{32,192},{40,200},{48,208},{56,2... | collective-permute-start | bytes 405512 | tf_op jit(solution)/shard_map/ppermute | solution.py:212
  70.2 2.0 %collective-permute-start.7 = (bf16[528,128]{1,0:T(8,128)(2,1)S(1)}, bf16[528,128]{1,0:T(8,128)(2,1)S(1)}, u32[]{:S(2)}, u32[]{:S(2)}) collective-permute-start(bf16[528,128]{1,0:T(8,128)(2,1)S(1)} %get-tuple-element.22), channel_id=1, source_target_pairs={{0,96},{8,104},{16,112},{24,120},{32,128},{40,136},{48,144},{56,15... | collective-permute-start | bytes 405512 | tf_op jit(solution)/shard_map/ppermute | solution.py:212
  72.2 4.6 %collective-permute-done.5.after_ref.refs_4_ = bf16[528,128]{1,0:T(8,128)(2,1)S(1)} collective-permute-done((bf16[528,128]{1,0:T(8,128)(2,1)S(1)}, bf16[528,128]{1,0:T(8,128)(2,1)S(1)}, u32[]{:S(2)}, u32[]{:S(2)}) %collective-permute-start.5) | collective-permute-done | bytes 135200 | tf_op jit(solution)/shard_map/ppermute | solution.py:212
  76.8 2.5 %far.9 = (bf16[528,128]{1,0:T(8,128)(2,1)S(1)}, bf16[528,128]{1,0:T(8,128)(2,1)S(1)}) custom-call(s32[1]{0:T(128)} %bitcast.home_ref, bf16[528,128]{1,0:T(8,128)(2,1)S(1)} %collective-permute-done.5.after_ref.refs_4_, bf16[8,512,128]{2,1,0:T(8,128)(2,1)S(1)} %all-to-all-done.1.query_ref, bf16[4,1536,128]{2,1,0:T(8,128)(2,1)S(1)} %get-tuple-element.17.key_ref, ...), custom_call_target="tpu_custom_call" | custom-call | flops 1 | bytes 1 | tf_op jit(solution)/shard_map/far/pallas_call | solution.py:310
  80.2 1.6 %collective-permute-start.8 = (bf16[528,128]{1,0:T(8,128)(2,1)S(1)}, bf16[528,128]{1,0:T(8,128)(2,1)S(1)}, u32[]{:S(2)}, u32[]{:S(2)}) collective-permute-start(bf16[528,128]{1,0:T(8,128)(2,1)S(1)} %get-tuple-element.23), channel_id=1, source_target_pairs={{0,64},{8,72},{16,80},{24,88},{32,96},{40,104},{48,112},{56,120},{... | collective-permute-start | bytes 405512 | tf_op jit(solution)/shard_map/ppermute | solution.py:212
  81.7 2.5 %far.7 = (bf16[528,128]{1,0:T(8,128)(2,1)S(1)}, bf16[528,128]{1,0:T(8,128)(2,1)S(1)}) custom-call(s32[1]{0:T(128)} %bitcast.home_ref, bf16[528,128]{1,0:T(8,128)(2,1)S(1)} %collective-permute-done.3.after_ref.refs_3_, bf16[8,512,128]{2,1,0:T(8,128)(2,1)S(1)} %all-to-all-done.1.query_ref, bf16[4,1536,128]{2,1,0:T(8,128)(2,1)S(1)} %get-tuple-element.17.key_ref, ...), custom_call_target="tpu_custom_call" | custom-call | flops 1 | bytes 1 | tf_op jit(solution)/shard_map/far/pallas_call | solution.py:310
  84.2 0.9 collective-permute-start.4
  85.2 3.4 %collective-permute-start.9 = (bf16[528,128]{1,0:T(8,128)(2,1)S(1)}, bf16[528,128]{1,0:T(8,128)(2,1)S(1)}, u32[]{:S(2)}, u32[]{:S(2)}) collective-permute-start(bf16[528,128]{1,0:T(8,128)(2,1)S(1)} %get-tuple-element.24), channel_id=1, source_target_pairs={{0,32},{8,40},{16,48},{24,56},{32,64},{40,72},{48,80},{56,88},{64,... | collective-permute-start | bytes 405512 | tf_op jit(solution)/shard_map/ppermute | solution.py:212
  88.6 1.4 %far.8.refs_0_ = bf16[528,128]{1,0:T(8,128)(2,1)S(1)} custom-call(s32[1]{0:T(128)} %bitcast.home_ref, bf16[528,128]{1,0:T(8,128)(2,1)S(1)} %get-tuple-element.20.after_ref, bf16[8,512,128]{2,1,0:T(8,128)(2,1)S(1)} %all-to-all-done.1.query_ref, bf16[4,1536,128]{2,1,0:T(8,128)(2,1)S(1)} %get-tuple-element.17.key_ref, bf16[4,1536,256]{2,1,0:T(8,128)(2,1)S(1)} %copy-done), custom_call_target="tpu_custom_call" | custom-call | flops 1 | bytes 1 | tf_op jit(solution)/shard_map/far/pallas_call | solution.py:310
  90.0 1.1 collective-permute-done.8.refs_6_
  91.1 1.3 %collective-permute-done.4.refs_1_ = bf16[528,128]{1,0:T(8,128)(2,1)S(1)} collective-permute-done((bf16[528,128]{1,0:T(8,128)(2,1)S(1)}, bf16[528,128]{1,0:T(8,128)(2,1)S(1)}, u32[]{:S(2)}, u32[]{:S(2)}) %collective-permute-start.4) | collective-permute-done | bytes 135200 | tf_op jit(solution)/shard_map/ppermute | solution.py:212
  92.4 1.0 collective-permute-done.9.refs_7_
  93.4 2.0 %combine.1 = bf16[2048,128]{1,0:T(8,128)(2,1)S(1)} custom-call(s32[1]{0:T(128)} %bitcast.home_ref, s32[128]{0:T(128)S(1)} %copy-done.10, f32[2048,128]{1,0:T(8,128)S(1)} %copy-done.6, f32[2048,128]{1,0:T(8,128)S(1)} %copy-done.2, bf16[528,128]{1,0:T(8,128)(2,1)S(1)} %far.8.refs_0_, bf16[528,128]{1,0:T(8,128)(2,1)S(1)} %collective-permute-done.4.refs_1_, ...), custom_call_target="tpu_custom_call" | custom-call | tf_op jit(solution)/shard_map/combine/pallas_call | solution.py:331
  95.4 14.0 %all_to_all.15 = bf16[8,16,16,128]{3,2,1,0:T(8,128)(2,1)S(1)} all-to-all(bf16[8,16,16,128]{3,2,1,0:T(8,128)(2,1)S(1)} %bitcast.16), channel_id=1, replica_groups=mesh['batch'=32,'head'=8] {'head'}, dimensions={0} | all-to-all | bytes 1048576 | tf_op jit(solution)/shard_map/all_to_all | solution.py:344
  (33 shorter events, 2.9 us)
Async XLA Ops:
  0.0 22.1 %collective-permute-start = (bf16[2,1536,128]{2,1,0:T(8,128)(2,1)}, bf16[2,1536,128]{2,1,0:T(8,128)(2,1)S(1)}, u32[]{:S(2)}, u32[]{:S(2)}) collective-permute-start(bf16[2,1536,128]{2,1,0:T(8,128)(2,1)} %bitcast.17), channel_id=1, source_target_pairs={{0,8},{8,16},{16,24},{24,0},{32,40},{40,48},{48,56},{56,32},{64,72... | collective-permute-start | bytes 2359304 | tf_op jit(solution)/shard_map/ppermute | solution.py:218
  2.0 20.1 %collective-permute-start.1 = (bf16[2,1536,128]{2,1,0:T(8,128)(2,1)}, bf16[2,1536,128]{2,1,0:T(8,128)(2,1)S(1)}, u32[]{:S(2)}, u32[]{:S(2)}) collective-permute-start(bf16[2,1536,128]{2,1,0:T(8,128)(2,1)} %bitcast.18), channel_id=1, source_target_pairs={{0,24},{8,0},{16,8},{24,16},{32,56},{40,32},{48,40},{56,48},{64,88... | collective-permute-start | bytes 2359304 | tf_op jit(solution)/shard_map/ppermute | solution.py:218
  3.3 1.0 copy-start.8
  5.9 26.6 %copy-start.12 = (bf16[128,2,2,128]{3,2,1,0:T(2,128)(2,1)S(1)}, bf16[128,2,2,128]{3,2,1,0:T(2,128)(2,1)}, u32[]{:S(2)}) copy-start(bf16[128,2,2,128]{3,2,1,0:T(2,128)(2,1)} %param.8) | copy-start | bytes 393220
  5.9 26.7 %copy-start.11 = (s32[128]{0:T(128)S(1)}, s32[128]{0:T(128)}, u32[]{:S(2)}) copy-start(s32[128]{0:T(128)} %len_ref.1) | copy-start | bytes 1540
  5.9 16.2 %all-to-all-start = ((bf16[8,16,16,128]{3,2,1,0:T(8,128)(2,1)}), bf16[8,16,16,128]{3,2,1,0:T(8,128)(2,1)S(1)}, u32[]{:S(2)}, u32[]{:S(2)}) async-start(bf16[8,16,16,128]{3,2,1,0:T(8,128)(2,1)} %split.1), calls=%async_computation | async-start | bytes 1048576 | tf_op jit(solution)/shard_map/all_to_all | solution.py:237
  22.1 10.5 %copy-start.3 = (bf16[2,1536,128]{2,1,0:T(8,128)(2,1)}, bf16[2,1536,128]{2,1,0:T(8,128)(2,1)S(1)}, u32[]{:S(2)}) copy-start(bf16[2,1536,128]{2,1,0:T(8,128)(2,1)S(1)} %collective-permute-done.1.right_ref.refs_1_) | copy-start | bytes 2359300
  22.1 0.7 copy-start.9
  24.9 36.7 %all-to-all-start.1 = ((bf16[8,512,128]{2,1,0:T(8,128)(2,1)}), bf16[8,512,128]{2,1,0:T(8,128)(2,1)S(1)}, u32[]{:S(2)}, u32[]{:S(2)}) async-start(bf16[8,512,128]{2,1,0:T(8,128)(2,1)} %bitcast.6), calls=%async_computation.1 | async-start | bytes 2097152 | tf_op jit(solution)/shard_map/all_to_all | solution.py:259
  32.4 19.1 %collective-permute-start.2 = (bf16[2,1536,128]{2,1,0:T(8,128)(2,1)S(1)}, bf16[2,1536,128]{2,1,0:T(8,128)(2,1)S(1)}, u32[]{:S(2)}, u32[]{:S(2)}) collective-permute-start(bf16[2,1536,128]{2,1,0:T(8,128)(2,1)S(1)} %collective-permute-done.left_ref.refs_3_), channel_id=1, source_target_pairs={{0,8},{8,16},{16,24},{24,0},{32,40},{40,48},{48,56},{56,32},{64,72... | collective-permute-start | bytes 2359304 | tf_op jit(solution)/shard_map/ppermute | solution.py:218
  32.6 18.9 %copy-start.4 = (bf16[2,1536,128]{2,1,0:T(8,128)(2,1)S(1)}, bf16[2,1536,128]{2,1,0:T(8,128)(2,1)}, u32[]{:S(2)}) copy-start(bf16[2,1536,128]{2,1,0:T(8,128)(2,1)} %copy-done.3) | copy-start | bytes 2359300
  32.6 18.9 %copy-start.7 = (bf16[1,2,1536,128]{3,2,1,0:T(8,128)(2,1)S(1)}, bf16[1,2,1536,128]{3,2,1,0:T(8,128)(2,1)}, u32[]{:S(2)}) copy-start(bf16[1,2,1536,128]{3,2,1,0:T(8,128)(2,1)} %param.10) | copy-start | bytes 2359300
  42.0 1.0 copy-start.1
  43.0 1.0 copy-start.5
  61.6 1.2 %copy-start.2 = (f32[2048,128]{1,0:T(8,128)S(1)}, f32[2048,128]{1,0:T(8,128)}, u32[]{:S(2)}) copy-start(f32[2048,128]{1,0:T(8,128)} %copy-done.1) | copy-start | bytes 3145732
  62.8 3.6 %copy-start = (bf16[4,1536,256]{2,1,0:T(8,128)(2,1)S(1)}, bf16[4,1536,256]{2,1,0:T(8,128)(2,1)}, u32[]{:S(2)}) copy-start(bf16[4,1536,256]{2,1,0:T(8,128)(2,1)} %get-tuple-element.18.wide_ref) | copy-start | bytes 9437188
  66.3 10.5 %collective-permute-start.5 = (bf16[528,128]{1,0:T(8,128)(2,1)S(1)}, bf16[528,128]{1,0:T(8,128)(2,1)S(1)}, u32[]{:S(2)}, u32[]{:S(2)}) collective-permute-start(bf16[528,128]{1,0:T(8,128)(2,1)S(1)} %far.5.after_ref), channel_id=1, source_target_pairs={{0,128},{8,136},{16,144},{24,152},{32,160},{40,168},{48,176},{56,1... | collective-permute-start | bytes 405512 | tf_op jit(solution)/shard_map/ppermute | solution.py:212
  68.9 12.9 %collective-permute-start.3 = (bf16[528,128]{1,0:T(8,128)(2,1)S(1)}, bf16[528,128]{1,0:T(8,128)(2,1)S(1)}, u32[]{:S(2)}, u32[]{:S(2)}) collective-permute-start(bf16[528,128]{1,0:T(8,128)(2,1)S(1)} %get-tuple-element.19), channel_id=1, source_target_pairs={{0,160},{8,168},{16,176},{24,184},{32,192},{40,200},{48,208},{56,2... | collective-permute-start | bytes 405512 | tf_op jit(solution)/shard_map/ppermute | solution.py:212
  70.2 19.8 %collective-permute-start.7 = (bf16[528,128]{1,0:T(8,128)(2,1)S(1)}, bf16[528,128]{1,0:T(8,128)(2,1)S(1)}, u32[]{:S(2)}, u32[]{:S(2)}) collective-permute-start(bf16[528,128]{1,0:T(8,128)(2,1)S(1)} %get-tuple-element.22), channel_id=1, source_target_pairs={{0,96},{8,104},{16,112},{24,120},{32,128},{40,136},{48,144},{56,15... | collective-permute-start | bytes 405512 | tf_op jit(solution)/shard_map/ppermute | solution.py:212
  79.3 10.8 %collective-permute-start.6 = (bf16[528,128]{1,0:T(8,128)(2,1)S(1)}, bf16[528,128]{1,0:T(8,128)(2,1)S(1)}, u32[]{:S(2)}, u32[]{:S(2)}) collective-permute-start(bf16[528,128]{1,0:T(8,128)(2,1)S(1)} %get-tuple-element.21), channel_id=1, source_target_pairs={{0,192},{8,200},{16,208},{24,216},{32,224},{40,232},{48,240},{56,2... | collective-permute-start | bytes 405512 | tf_op jit(solution)/shard_map/ppermute | solution.py:212
  80.2 10.9 %collective-permute-start.8 = (bf16[528,128]{1,0:T(8,128)(2,1)S(1)}, bf16[528,128]{1,0:T(8,128)(2,1)S(1)}, u32[]{:S(2)}, u32[]{:S(2)}) collective-permute-start(bf16[528,128]{1,0:T(8,128)(2,1)S(1)} %get-tuple-element.23), channel_id=1, source_target_pairs={{0,64},{8,72},{16,80},{24,88},{32,96},{40,104},{48,112},{56,120},{... | collective-permute-start | bytes 405512 | tf_op jit(solution)/shard_map/ppermute | solution.py:212
  84.2 9.2 %copy-start.6 = (f32[2048,128]{1,0:T(8,128)S(1)}, f32[2048,128]{1,0:T(8,128)}, u32[]{:S(2)}) copy-start(f32[2048,128]{1,0:T(8,128)} %copy-done.5) | copy-start | bytes 3145732
  84.2 9.2 %copy-start.10 = (s32[128]{0:T(128)S(1)}, s32[128]{0:T(128)}, u32[]{:S(2)}) copy-start(s32[128]{0:T(128)} %slots.1.slot_ref) | copy-start | bytes 1540
  84.2 8.2 %collective-permute-start.4 = (bf16[528,128]{1,0:T(8,128)(2,1)S(1)}, bf16[528,128]{1,0:T(8,128)(2,1)S(1)}, u32[]{:S(2)}, u32[]{:S(2)}) collective-permute-start(bf16[528,128]{1,0:T(8,128)(2,1)S(1)} %get-tuple-element.20.after_ref), channel_id=1, source_target_pairs={{0,224},{8,232},{16,240},{24,248},{32,0},{40,8},{48,16},{56,24},{6... | collective-permute-start | bytes 405512 | tf_op jit(solution)/shard_map/ppermute | solution.py:212
  85.2 8.3 %collective-permute-start.9 = (bf16[528,128]{1,0:T(8,128)(2,1)S(1)}, bf16[528,128]{1,0:T(8,128)(2,1)S(1)}, u32[]{:S(2)}, u32[]{:S(2)}) collective-permute-start(bf16[528,128]{1,0:T(8,128)(2,1)S(1)} %get-tuple-element.24), channel_id=1, source_target_pairs={{0,32},{8,40},{16,48},{24,56},{32,64},{40,72},{48,80},{56,88},{64,... | collective-permute-start | bytes 405512 | tf_op jit(solution)/shard_map/ppermute | solution.py:212
